TPU v7x, 32 devices: a whole 2x2x4 slice. The times are simulated.
32 devices in a mesh: rep: 2 (over core), dp: 4 (over y, x), expert: 4 (over z).
Axes of the slice: x: 2, y: 2, z: 4, core: 2. Of those that a mesh axis runs over, the one named last changes fastest.
Arguments:
- tokens: bfloat16 [32768, 768], P(('rep', 'dp', 'expert')), may hold values from -6 to 6
- routes: int32 [32768, 2], P(('rep', 'dp', 'expert')), may hold values from 0 to 7, all different within a row; in each aligned block of 1024 rows (0 to 1023, 1024 to 2047, ...) at most 384 rows name the same one
- cotangent: bfloat16 [32768, 768], P(('rep', 'dp', 'expert')), may hold values from -6 to 6
- w_query: bfloat16 [768, 768], P('dp'), may hold values from -0.21875 to 0.21875
- w_key: bfloat16 [768, 768], P('dp'), may hold values from -0.21875 to 0.21875
- w_value: bfloat16 [768, 768], P('dp'), may hold values from -0.21875 to 0.21875
- w_out: bfloat16 [768, 768], P('dp'), may hold values from -0.875 to 0.875
- w_router: bfloat16 [768, 8], P('dp'), may hold values from -0.15625 to 0.15625
- gain_attn: bfloat16 [768], P('dp'), may hold values from 0.099609375 to 1.8984375
- gain_moe: bfloat16 [768], P('dp'), may hold values from 0.099609375 to 1.8984375
- bias_table: bfloat16 [32, 12], P('dp'), may hold values from -4 to 4
- expert_up: bfloat16 [8, 768, 3072], P('expert', None, 'dp'), may hold values from -0.21875 to 0.21875
- expert_down: bfloat16 [8, 3072, 768], P('expert', 'dp'), may hold values from -0.21875 to 0.21875
Outputs:
- output: bfloat16 [32768, 768], P(('rep', 'dp', 'expert'))
- grad_tokens: float32 [32768, 768], P(('rep', 'dp', 'expert'))
- grad_query: float32 [768, 768], P('dp')
- grad_key: float32 [768, 768], P('dp')
- grad_value: float32 [768, 768], P('dp')
- grad_out: float32 [768, 768], P('dp')
- grad_router: float32 [768, 8], P('dp')
- grad_gain_attn: float32 [768], P('dp')
- grad_gain_moe: float32 [768], P('dp')
- grad_table: float32 [32, 12], P('dp')
- grad_up: float32 [8, 768, 3072], P('expert', None, 'dp')
- grad_down: float32 [8, 3072, 768], P('expert', 'dp')
Inputs may be any that keep to these rules, and one draw needn't show every extreme that they name: `routes`: each row names 2 different experts; among the 1024 rows of one sequence no expert is named more than 384 times, a bound that some block reaches; every expert is named somewhere.
All inputs are finite; a program needn't handle non-finite values.
Results may differ from a plain program's by a relative error of at most 0.019.
Values may be sent and summed in bfloat16 or wider, within the bound.
A program may use at most 384 MiB of HBM per device.

v0:
```python
import jax
import jax.numpy as jnp
from jax import lax
from jax.sharding import PartitionSpec as P

distance_edges = (18, 21, 24, 27, 31, 35, 40, 45, 51, 58, 66, 75, 85, 97, 110)


def bucket_ids(distance):
    distance = jnp.maximum(distance, 0)
    result = jnp.minimum(distance, 16)
    for edge_value in distance_edges:
        result = result + (distance >= edge_value).astype(jnp.int32)
    return result


def rms_apply(values, gain_vec):
    return values * lax.rsqrt(jnp.mean(values * values, axis=-1, keepdims=True) + 1e-06) * gain_vec


def gelu_exact(values):
    return jax.nn.gelu(values, approximate=False)


def slot_targets(route_rows, expert_count, capacity):
    flat_routes = route_rows.reshape(-1)
    one_hot = (flat_routes[:, None] == jnp.arange(expert_count, dtype=jnp.int32)[None, :]).astype(
        jnp.int32
    )
    earlier = jnp.cumsum(one_hot, axis=0) - one_hot
    return flat_routes * capacity + jnp.sum(earlier * one_hot, axis=1)


def slot_sources(targets, slot_count):
    pick_ids = jnp.arange(targets.shape[0], dtype=jnp.int32)
    source_ids = jnp.zeros((slot_count,), jnp.int32).at[targets].set(pick_ids)
    occupied = jnp.zeros((slot_count,), jnp.int32).at[targets].set(1)
    return (source_ids, occupied)


def bias_rows(table_full, begin_row, block_rows, key_count):
    row_pos = begin_row + jnp.arange(block_rows, dtype=jnp.int32)
    col_pos = jnp.arange(key_count, dtype=jnp.int32)
    distance = row_pos[:, None] - col_pos[None, :]
    bucket_range = jnp.arange(table_full.shape[0], dtype=jnp.int32)
    one_hot = (bucket_ids(distance).reshape(-1)[:, None] == bucket_range[None, :]).astype(
        jnp.bfloat16
    )
    position_bias = jnp.einsum("nk,kh->hn", one_hot, table_full, preferred_element_type=jnp.float32)
    return (
        one_hot,
        position_bias.reshape(table_full.shape[1], block_rows, key_count),
        distance >= 0,
    )


def block_scores(queries, key_part, table_full, begin_row, block_rows, score_scale):
    key_count = key_part.shape[0]
    one_hot, position_bias, causal = bias_rows(table_full, begin_row, block_rows, key_count)
    query_block = queries[begin_row : begin_row + block_rows]
    scores = (
        jnp.einsum("ihd,jhd->hij", query_block, key_part, preferred_element_type=jnp.float32)
        * score_scale
        + position_bias
    )
    return (jnp.where(causal[None], scores, -1e30), one_hot, query_block)


def local(
    tokens,
    routes,
    cotangent,
    w_query,
    w_key,
    w_value,
    w_out,
    w_router,
    gain_attn,
    gain_moe,
    bias_table,
    expert_up,
    expert_down,
):
    highest = lax.Precision.HIGHEST
    query_full, key_full, value_full, out_full, router_full, gain_one, gain_two, table_full = (
        lax.all_gather(w_query, "dp", axis=0, tiled=True),
        lax.all_gather(w_key, "dp", axis=0, tiled=True),
        lax.all_gather(w_value, "dp", axis=0, tiled=True),
        lax.all_gather(w_out, "dp", axis=0, tiled=True),
        lax.all_gather(w_router, "dp", axis=0, tiled=True),
        lax.all_gather(gain_attn, "dp", axis=0, tiled=True),
        lax.all_gather(gain_moe, "dp", axis=0, tiled=True),
        lax.all_gather(bias_table, "dp", axis=0, tiled=True),
    )
    seq_len, model_width = tokens.shape
    head_count = table_full.shape[1]
    head_dim = model_width // head_count
    local_experts = expert_up.shape[0]
    groups = lax.axis_size("expert")
    quarters = lax.axis_size("dp")
    expert_count = groups * local_experts
    top_count = routes.shape[1]
    capacity = 3 * seq_len * top_count // (2 * expert_count)
    block_rows = min(512, seq_len)
    block_total = seq_len // block_rows
    score_scale = head_dim ** (-0.5)
    inputs = tokens.astype(jnp.float32)
    norm_one, pull_one = jax.vjp(rms_apply, inputs, gain_one.astype(jnp.float32))
    norm_one_bf = norm_one.astype(jnp.bfloat16)
    queries = (
        jnp.dot(norm_one_bf, query_full, preferred_element_type=jnp.float32)
        .astype(jnp.bfloat16)
        .reshape(seq_len, head_count, head_dim)
    )
    key_rows = (
        jnp.dot(norm_one_bf, key_full, preferred_element_type=jnp.float32)
        .astype(jnp.bfloat16)
        .reshape(seq_len, head_count, head_dim)
    )
    value_rows = (
        jnp.dot(norm_one_bf, value_full, preferred_element_type=jnp.float32)
        .astype(jnp.bfloat16)
        .reshape(seq_len, head_count, head_dim)
    )
    out_blocks = []
    log_sums = []
    for block_index in range(block_total):
        begin_row = block_index * block_rows
        end_row = begin_row + block_rows
        scores, one_hot, query_block = block_scores(
            queries, key_rows[:end_row], table_full, begin_row, block_rows, score_scale
        )
        row_max = jnp.max(scores, axis=-1, keepdims=True)
        exp_scores = jnp.exp(scores - row_max)
        row_total = jnp.sum(exp_scores, axis=-1, keepdims=True)
        prob_bf = (exp_scores / row_total).astype(jnp.bfloat16)
        out_blocks.append(
            jnp.einsum(
                "hij,jhd->ihd", prob_bf, value_rows[:end_row], preferred_element_type=jnp.float32
            )
        )
        log_sums.append(row_max + jnp.log(row_total))
    attn_bf = jnp.concatenate(out_blocks, axis=0).astype(jnp.bfloat16).reshape(seq_len, model_width)
    middle = inputs + jnp.dot(attn_bf, out_full, preferred_element_type=jnp.float32)
    norm_two, pull_two = jax.vjp(rms_apply, middle, gain_two.astype(jnp.float32))
    norm_two_bf = norm_two.astype(jnp.bfloat16)
    logits = jnp.dot(norm_two_bf, router_full, preferred_element_type=jnp.float32)
    gate_vals = jax.nn.softmax(jnp.take_along_axis(logits, routes, axis=1), axis=-1)
    targets = slot_targets(routes, expert_count, capacity)
    source_ids, occupied = slot_sources(targets, expert_count * capacity)
    send_rows = jnp.where(
        occupied[:, None] > 0, norm_two_bf[source_ids // top_count], jnp.zeros((), jnp.bfloat16)
    )
    received = lax.all_to_all(
        send_rows.reshape(groups, local_experts, capacity, model_width),
        "expert",
        split_axis=0,
        concat_axis=2,
        tiled=True,
    )
    expert_in = received.reshape(local_experts, groups * capacity, model_width)
    up_full, down_full = (
        lax.all_gather(expert_up, "dp", axis=2, tiled=True),
        lax.all_gather(expert_down, "dp", axis=1, tiled=True),
    )
    pre_act = jnp.einsum("erd,edf->erf", expert_in, up_full, preferred_element_type=jnp.float32)
    hidden_bf = gelu_exact(pre_act).astype(jnp.bfloat16)
    part_width = hidden_bf.shape[2] // quarters
    out_total = jnp.zeros((local_experts, expert_in.shape[1], model_width), jnp.float32)
    for part_index in range(quarters):
        hidden_part = hidden_bf[:, :, part_index * part_width : (part_index + 1) * part_width]
        down_part = down_full[:, part_index * part_width : (part_index + 1) * part_width, :]
        part_term = jnp.einsum(
            "erf,efd->erd", hidden_part, down_part, preferred_element_type=jnp.float32
        )
        out_total = out_total + part_term.astype(jnp.bfloat16).astype(jnp.float32)
    expert_out = out_total.astype(jnp.bfloat16)
    returned = lax.all_to_all(
        expert_out.reshape(local_experts, groups, capacity, model_width),
        "expert",
        split_axis=1,
        concat_axis=0,
        tiled=True,
    )
    returned = returned.reshape(expert_count * capacity, model_width)
    picked = returned[targets].reshape(seq_len, top_count, model_width).astype(jnp.float32)
    output = (middle + jnp.sum(gate_vals[:, :, None] * picked, axis=1)).astype(jnp.bfloat16)
    grad_output = cotangent.astype(jnp.float32)
    grad_gates = jnp.sum(grad_output[:, None, :] * picked, axis=-1)
    grad_chosen = gate_vals * (grad_gates - jnp.sum(gate_vals * grad_gates, axis=-1, keepdims=True))
    expert_range = jnp.arange(expert_count, dtype=jnp.int32)
    grad_logits = jnp.sum(
        jnp.where(routes[:, :, None] == expert_range[None, None, :], grad_chosen[:, :, None], 0.0),
        axis=1,
    )
    grad_router_local = jnp.einsum(
        "td,te->de", norm_two_bf.astype(jnp.float32), grad_logits, precision=highest
    )
    grad_norm_router = jnp.einsum(
        "te,de->td", grad_logits, router_full.astype(jnp.float32), precision=highest
    )
    weighted = (
        (gate_vals[:, :, None] * grad_output[:, None, :])
        .reshape(seq_len * top_count, model_width)
        .astype(jnp.bfloat16)
    )
    grad_send = jnp.where(occupied[:, None] > 0, weighted[source_ids], jnp.zeros((), jnp.bfloat16))
    grad_expert_out = lax.all_to_all(
        grad_send.reshape(groups, local_experts, capacity, model_width),
        "expert",
        split_axis=0,
        concat_axis=2,
        tiled=True,
    )
    grad_expert_out = grad_expert_out.reshape(local_experts, groups * capacity, model_width)
    grad_hidden = jnp.einsum(
        "erd,efd->erf", grad_expert_out, down_full, preferred_element_type=jnp.float32
    )
    unused_value, pull_gelu = jax.vjp(gelu_exact, pre_act)
    grad_pre = pull_gelu(grad_hidden)[0].astype(jnp.bfloat16)
    grad_up_local = jnp.einsum(
        "erd,erf->edf", expert_in, grad_pre, preferred_element_type=jnp.float32
    )
    grad_down_local = jnp.einsum(
        "erf,erd->efd", hidden_bf, grad_expert_out, preferred_element_type=jnp.float32
    )
    part_width = grad_pre.shape[2] // quarters
    grad_total = jnp.zeros((local_experts, grad_pre.shape[1], model_width), jnp.float32)
    for part_index in range(quarters):
        grad_pre_part = grad_pre[:, :, part_index * part_width : (part_index + 1) * part_width]
        up_part = up_full[:, :, part_index * part_width : (part_index + 1) * part_width]
        grad_term = jnp.einsum(
            "erf,edf->erd", grad_pre_part, up_part, preferred_element_type=jnp.float32
        )
        grad_total = grad_total + grad_term.astype(jnp.bfloat16).astype(jnp.float32)
    grad_expert_in = grad_total.astype(jnp.bfloat16)
    grad_up_local, grad_down_local = (
        lax.psum_scatter(
            grad_up_local.astype(jnp.bfloat16), "dp", scatter_dimension=2, tiled=True
        ).astype(jnp.float32),
        lax.psum_scatter(
            grad_down_local.astype(jnp.bfloat16), "dp", scatter_dimension=1, tiled=True
        ).astype(jnp.float32),
    )
    grad_up_sum, grad_down_sum = (
        lax.psum(grad_up_local.astype(jnp.bfloat16), "rep").astype(jnp.float32),
        lax.psum(grad_down_local.astype(jnp.bfloat16), "rep").astype(jnp.float32),
    )
    grad_back = lax.all_to_all(
        grad_expert_in.reshape(local_experts, groups, capacity, model_width),
        "expert",
        split_axis=1,
        concat_axis=0,
        tiled=True,
    )
    grad_back = grad_back.reshape(expert_count * capacity, model_width)
    grad_norm_two = (
        jnp.sum(
            grad_back[targets].reshape(seq_len, top_count, model_width).astype(jnp.float32), axis=1
        )
        + grad_norm_router
    )
    grad_middle_part, grad_gain_two = pull_two(grad_norm_two)
    grad_middle = grad_output + grad_middle_part
    grad_attn_bf = grad_middle.astype(jnp.bfloat16)
    grad_out_local = jnp.einsum(
        "tc,td->cd", attn_bf, grad_attn_bf, preferred_element_type=jnp.float32
    )
    grad_heads = (
        jnp.einsum("td,cd->tc", grad_attn_bf, out_full, preferred_element_type=jnp.float32)
        .astype(jnp.bfloat16)
        .reshape(seq_len, head_count, head_dim)
    )
    query_grad_blocks = []
    grad_key_total = jnp.zeros((seq_len, head_count, head_dim), jnp.float32)
    grad_value_total = jnp.zeros((seq_len, head_count, head_dim), jnp.float32)
    grad_table_total = jnp.zeros(table_full.shape, jnp.float32)
    for block_index in range(block_total):
        begin_row = block_index * block_rows
        end_row = begin_row + block_rows
        key_part = key_rows[:end_row]
        value_part = value_rows[:end_row]
        scores, one_hot, query_block = block_scores(
            queries, key_part, table_full, begin_row, block_rows, score_scale
        )
        probs = jnp.exp(scores - log_sums[block_index])
        prob_bf = probs.astype(jnp.bfloat16)
        grad_block = grad_heads[begin_row:end_row]
        grad_probs = jnp.einsum(
            "ihd,jhd->hij", grad_block, value_part, preferred_element_type=jnp.float32
        )
        grad_scores = probs * (grad_probs - jnp.sum(probs * grad_probs, axis=-1, keepdims=True))
        grad_scores_bf = grad_scores.astype(jnp.bfloat16)
        query_grad_blocks.append(
            jnp.einsum("hij,jhd->ihd", grad_scores_bf, key_part, preferred_element_type=jnp.float32)
            * score_scale
        )
        grad_key_total = grad_key_total.at[:end_row].add(
            jnp.einsum(
                "hij,ihd->jhd", grad_scores_bf, query_block, preferred_element_type=jnp.float32
            )
            * score_scale
        )
        grad_value_total = grad_value_total.at[:end_row].add(
            jnp.einsum("hij,ihd->jhd", prob_bf, grad_block, preferred_element_type=jnp.float32)
        )
        grad_table_total = grad_table_total + jnp.einsum(
            "hn,nk->kh",
            grad_scores_bf.reshape(head_count, -1),
            one_hot,
            preferred_element_type=jnp.float32,
        )
    grad_queries = (
        jnp.concatenate(query_grad_blocks, axis=0)
        .astype(jnp.bfloat16)
        .reshape(seq_len, model_width)
    )
    grad_keys = grad_key_total.astype(jnp.bfloat16).reshape(seq_len, model_width)
    grad_values = grad_value_total.astype(jnp.bfloat16).reshape(seq_len, model_width)
    grad_query_local = jnp.einsum(
        "tc,td->cd", norm_one_bf, grad_queries, preferred_element_type=jnp.float32
    )
    grad_key_local = jnp.einsum(
        "tc,td->cd", norm_one_bf, grad_keys, preferred_element_type=jnp.float32
    )
    grad_value_local = jnp.einsum(
        "tc,td->cd", norm_one_bf, grad_values, preferred_element_type=jnp.float32
    )
    grad_norm_one = jnp.einsum(
        "td,cd->tc", grad_queries, query_full, preferred_element_type=jnp.float32
    )
    grad_norm_one = grad_norm_one + jnp.einsum(
        "td,cd->tc", grad_keys, key_full, preferred_element_type=jnp.float32
    )
    grad_norm_one = grad_norm_one + jnp.einsum(
        "td,cd->tc", grad_values, value_full, preferred_element_type=jnp.float32
    )
    grad_input_part, grad_gain_one = pull_one(grad_norm_one)
    grad_tokens = grad_middle + grad_input_part
    dense_shares = (
        lax.psum_scatter(
            grad_query_local.astype(jnp.bfloat16), "dp", scatter_dimension=0, tiled=True
        ).astype(jnp.float32),
        lax.psum_scatter(
            grad_key_local.astype(jnp.bfloat16), "dp", scatter_dimension=0, tiled=True
        ).astype(jnp.float32),
        lax.psum_scatter(
            grad_value_local.astype(jnp.bfloat16), "dp", scatter_dimension=0, tiled=True
        ).astype(jnp.float32),
        lax.psum_scatter(
            grad_out_local.astype(jnp.bfloat16), "dp", scatter_dimension=0, tiled=True
        ).astype(jnp.float32),
        lax.psum_scatter(
            grad_router_local.astype(jnp.bfloat16), "dp", scatter_dimension=0, tiled=True
        ).astype(jnp.float32),
        lax.psum_scatter(
            grad_gain_one.astype(jnp.bfloat16), "dp", scatter_dimension=0, tiled=True
        ).astype(jnp.float32),
        lax.psum_scatter(
            grad_gain_two.astype(jnp.bfloat16), "dp", scatter_dimension=0, tiled=True
        ).astype(jnp.float32),
        lax.psum_scatter(
            grad_table_total.astype(jnp.bfloat16), "dp", scatter_dimension=0, tiled=True
        ).astype(jnp.float32),
    )
    dense_sums = lax.psum(
        (
            dense_shares[0],
            dense_shares[1],
            dense_shares[2],
            dense_shares[3],
            dense_shares[4],
            dense_shares[5],
            dense_shares[6],
            dense_shares[7],
        ),
        ("rep", "expert"),
    )
    return (
        output,
        grad_tokens,
        dense_sums[0],
        dense_sums[1],
        dense_sums[2],
        dense_sums[3],
        dense_sums[4],
        dense_sums[5],
        dense_sums[6],
        dense_sums[7],
        grad_up_sum,
        grad_down_sum,
    )


def solution(mesh):
    placed = (
        P(("rep", "dp", "expert"), None),
        P(("rep", "dp", "expert"), None),
        P(("rep", "dp", "expert"), None),
        P("dp", None),
        P("dp", None),
        P("dp", None),
        P("dp", None),
        P("dp", None),
        P("dp"),
        P("dp"),
        P("dp", None),
        P("expert", None, "dp"),
        P("expert", "dp", None),
    )
    return jax.shard_map(
        local,
        mesh=mesh,
        in_specs=placed,
        out_specs=(
            P(("rep", "dp", "expert"), None),
            P(("rep", "dp", "expert"), None),
            P("dp", None),
            P("dp", None),
            P("dp", None),
            P("dp", None),
            P("dp", None),
            P("dp"),
            P("dp"),
            P("dp", None),
            P("expert", None, "dp"),
            P("expert", "dp", None),
        ),
        check_vma=False,
    )
```

profile of v0, /device:TPU:1, one launch (start us, length us, event | category | flops | bytes accessed | tf_op | source)
XLA Modules:
  0.0 1418.0 jit_solution(8464809042659766483)
XLA Ops:
  26.2 8.8 all-reduce.9
  57.2 8.1 scatter_custom_fusion.1
  65.3 8.3 scatter_custom_fusion
  98.1 8.5 mul.272
  121.8 19.5 %copy.272 = f32[2,8,512,512]{3,2,1,0:T(8,128)} copy(f32[2,8,512,512]{3,1,2,0:T(8,128)S(1)} %bitcast.189) | data formatting | bytes 33554432
  141.3 11.3 slice.237
  152.7 12.9 copy.222
  169.5 17.3 %fusion.1 = f32[524288,12]{0,1:T(8,128)} fusion(bf16[32,12]{1,0:T(8,128)(2,1)S(1)} %all_gather.34, s32[524288]{0:T(1024)S(1)} %add_add_fusion.3), kind=kOutput, calls=%fused_computation.9 | convolution fusion | flops 419430400 | bytes 27263744 | tf_op jit(solution)/shard_map/nk,kh->hn/dot_general | solution.py:49
  186.8 32.1 %copy.278 = f32[2,8,512,1024]{3,2,1,0:T(8,128)} copy(f32[2,8,512,1024]{3,1,2,0:T(8,128)} %bitcast.187) | data formatting | bytes 67108864
  246.6 16.2 %fusion.144 = (f32[12,512]{1,0:T(8,128)S(1)}, f32[12,512,1024]{2,1,0:T(8,128)}) fusion(f32[16,512,1024]{2,1,0:T(8,128)} %bitcast.188, bf16[512,12,64]{0,2,1:T(8,128)(2,1)} %bitcast.201, bf16[1024,12,64]{0,2,1:T(8,128)(2,1)S(1)} %bitcast.200, pred[512,1024]{1,0:T(8,128)(4,1)} %get-tuple-element.197), kind=kOutput, calls=%fused_computation.250 | convolution fusion | flops 830466048 | bytes 53239808 | tf_op jit(solution)/shard_map/ihd,jhd->hij/dot_general | solution.py:62
  262.8 11.0 fusion.13
  273.9 11.3 fusion.90
  292.4 12.8 gather_fusion.4
  312.5 17.0 %gather_fusion.2 = bf16[3072,768]{1,0:T(8,128)(2,1)} fusion(bf16[2048,768]{1,0:T(8,128)(2,1)} %multiply_convert_fusion.3, s32[3072]{0:T(1024)S(1)} %copy-done.76), kind=kCustom, calls=%fused_computation.2 | custom fusion | bytes 9449472 | tf_op jit(solution)/shard_map/gather | solution.py:207
  329.5 13.6 gather_fusion
  349.9 106.5 %all_to_all.60 = bf16[4,2,384,768]{3,2,1,0:T(8,128)(2,1)} all-to-all(bf16[4,2,384,768]{3,2,1,0:T(8,128)(2,1)S(1)} %get-tuple-element.195), channel_id=1, replica_groups=mesh['rep'=2,'dp'=4,'expert'=4] {'expert'}, dimensions={0} | all-to-all | bytes 9437184 | tf_op jit(solution)/shard_map/all_to_all | solution.py:208
  466.7 98.5 %all-to-all-done = bf16[4,2,384,768]{3,2,1,0:T(8,128)(2,1)} async-done(((bf16[4,2,384,768]{3,2,1,0:T(8,128)(2,1)}), bf16[4,2,384,768]{3,2,1,0:T(8,128)(2,1)}, u32[]{:S(2)}, u32[]{:S(2)}) %all-to-all-start) | async-done | bytes 4718624 | tf_op jit(solution)/shard_map/all_to_all | solution.py:154
  570.1 42.9 %fusion.24 = (u8[1536,3072]{1,0:T(8,128)(4,1)}, u8[1536,3072]{1,0:T(8,128)(4,1)}, f32[2,1536,3072]{2,1,0:T(8,128)}) fusion(bf16[2,1536,768]{2,1,0:T(8,128)(2,1)} %bitcast.219, bf16[2,768,3072]{2,1,0:T(8,128)(2,1)} %all-gather.16.cloned.1.call-done), kind=kOutput, calls=%fused_computation.61 | convolution fusion | flops 14608760832 | bytes 61341696 | tf_op jit(solution)/shard_map/erd,edf->erf/dot_general | solution.py:166
  613.0 89.6 %multiply_convert_fusion = (bf16[2,1536,3072]{2,1,0:T(8,128)(2,1)}, f32[2,1536,3072]{2,1,0:T(8,128)}) fusion(f32[2,1536,3072]{2,1,0:T(8,128)} %get-tuple-element.210, u8[1536,3072]{1,0:T(8,128)(4,1)} %get-tuple-element.161, u8[1536,3072]{1,0:T(8,128)(4,1)} %get-tuple-element.160), kind=kLoop, calls=%fused_computation.18 | loop fusion | flops 660602880 | bytes 103809024 | tf_op jit(solution)/shard_map/convert_element_type | solution.py:167
  702.6 20.9 %convolution_convert_fusion.1 = bf16[2,3072,768]{2,1,0:T(8,128)(2,1)} fusion(bf16[2,1536,3072]{2,1,0:T(8,128)(2,1)} %get-tuple-element.185, bf16[2,1536,768]{2,1,0:T(8,128)(2,1)S(1)} %bitcast.222), kind=kOutput, calls=%fused_computation.63 | convolution fusion | flops 14500233216 | bytes 33030144 | tf_op jit(solution)/shard_map/erf,erd->efd/dot_general | solution.py:224
  723.6 42.0 %add_convert_fusion = bf16[2,1536,3072]{2,1,0:T(8,128)(2,1)} fusion(f32[2,1536,3072]{2,1,0:T(8,128)} %get-tuple-element.186, f32[2,1536,3072]{2,1,0:T(8,128)} %get-tuple-element.210, bf16[2,1536,768]{2,1,0:T(8,128)(2,1)} %bitcast.221, bf16[2,3072,768]{2,1,0:T(8,128)(2,1)} %all-gather.18.cloned.1.call-done), kind=kOutput, calls=%fused_computation.17 | convolution fusion | flops 14627635200 | bytes 108527616 | tf_op jit(solution)/shard_map/erd,efd->erf/dot_general | solution.py:216
  765.6 9.7 fusion.29
  776.4 7.2 fusion.31
  783.6 7.2 fusion.33
  790.8 12.0 add_convert_fusion.1
  810.3 21.7 %convolution_convert_fusion = bf16[2,768,3072]{2,1,0:T(8,128)(2,1)} fusion(bf16[2,1536,768]{2,1,0:T(8,128)(2,1)} %bitcast.220, bf16[2,1536,3072]{2,1,0:T(8,128)(2,1)} %add_convert_fusion), kind=kOutput, calls=%fused_computation.62 | convolution fusion | flops 14500233216 | bytes 33030144 | tf_op jit(solution)/shard_map/erd,erf->edf/dot_general | solution.py:221
  832.1 9.3 fusion.37
  841.4 8.5 fusion.39
  849.9 8.0 fusion.41
  857.9 12.4 add_convert_fusion.2
  872.8 41.4 %all-to-all-done.3 = bf16[2,4,384,768]{3,2,0,1:T(8,128)(2,1)} async-done(((bf16[2,4,384,768]{3,2,0,1:T(8,128)(2,1)}), bf16[2,4,384,768]{3,2,0,1:T(8,128)(2,1)}, u32[]{:S(2)}, u32[]{:S(2)}) %all-to-all-start.3) | async-done | bytes 4718624 | tf_op jit(solution)/shard_map/all_to_all | solution.py:249
  919.4 11.9 gather_fusion.3
  935.9 10.3 reduce_sum.179
  948.5 74.6 %all-to-all-done.1 = bf16[2,4,384,768]{3,2,0,1:T(8,128)(2,1)} async-done(((bf16[2,4,384,768]{3,2,0,1:T(8,128)(2,1)}), bf16[2,4,384,768]{3,2,0,1:T(8,128)(2,1)}, u32[]{:S(2)}, u32[]{:S(2)}) %all-to-all-start.1) | async-done | bytes 4718624 | tf_op jit(solution)/shard_map/all_to_all | solution.py:178
  1023.1 13.0 gather_fusion.1
  1036.1 8.1 reshape.749
  1044.3 17.2 %multiply_reduce_fusion.2 = (f32[1024,2]{1,0:T(8,128)}, f32[1024,768]{1,0:T(8,128)}) fusion(f32[1024,2,768]{2,1,0:T(2,128)} %reshape.749, f32[1024,768]{1,0:T(8,128)S(1)} %copy-done.6, f32[1024,2]{1,0:T(8,128)} %copy-done.36), kind=kLoop, calls=%fused_computation.66 | loop fusion | flops 5502976 | bytes 12599296 | tf_op jit(solution)/shard_map/reduce_sum | solution.py:189
  1084.0 11.0 fusion.57
  1103.6 9.1 multiply_reduce_fusion.1
  1112.7 18.2 %multiply_reduce_fusion = (f32[12,512]{1,0:T(8,128)S(1)}, f32[12,512,1024]{2,1,0:T(8,128)}) fusion(f32[12,512,1024]{2,1,0:T(8,128)} %get-tuple-element.205, f32[12,512]{1,0:T(8,128)S(1)} %log_add_fusion, bf16[512,12,64]{0,2,1:T(8,128)(2,1)S(1)} %bitcast.216, bf16[1024,12,64]{0,2,1:T(8,128)(2,1)} %bitcast.230), kind=kOutput, calls=%fused_computation.39 | convolution fusion | flops 824174592 | bytes 52740096 | tf_op jit(solution)/shard_map/ihd,jhd->hij/dot_general | solution.py:289
  1131.0 18.6 %multiply_convert_fusion.1 = bf16[12,512,1024]{2,1,0:T(8,128)(2,1)S(1)} fusion(f32[12,512,1024]{2,1,0:T(8,128)} %get-tuple-element.213, f32[12,512,1024]{2,1,0:T(8,128)} %get-tuple-element.205, f32[12,512]{1,0:T(8,128)S(1)} %get-tuple-element.212, f32[12,512]{1,0:T(8,128)S(1)} %log_add_fusion), kind=kLoop, calls=%fused_computation.38 | loop fusion | flops 25165824 | bytes 62963712 | tf_op jit(solution)/shard_map/convert_element_type | solution.py:293
  1151.5 12.5 multiply_convert_fusion.2
  1194.0 9.0 copy.250
  1211.3 11.4 copy.280
  1240.3 29.2 %copy.281 = bf16[2,8,512,1024]{3,1,2,0:T(8,128)(2,1)S(1)} copy(bf16[2,8,512,1024]{3,2,1,0:T(8,128)(2,1)S(1)} %bitcast.190) | data formatting | bytes 33554432
  1269.6 10.0 fusion
  1285.3 13.1 all-reduce.8
  1299.4 104.9 %all-reduce.15 = (f32[192,768]{1,0:T(8,128)}, f32[192,768]{1,0:T(8,128)}, f32[192,768]{1,0:T(8,128)}, f32[192,768]{1,0:T(8,128)}, f32[192,8]{0,1:T(8,128)}, /*in...) all-reduce(bf16[192,768]{1,0:T(8,128)(2,1)} %reduce-scatter.10.clon, ...), channel_id=1, replica_groups=mesh['rep'=2,'dp'=4,'expert'=4] {'rep','expert'}, use_global_device_ids=true, to_apply=%region_23.24 | all-reduce | flops 591840 | bytes 3552000 | tf_op jit(solution)/shard_map/psum | solution.py:366
  (394 shorter events, 272.1 us)
Async XLA Ops:
  7.2 211.7 %all-gather.12.cloned.1.call-start = ((), (), s32[]{:S(2)}) async-start(), calls=%async_computation.13 | async-start | bytes 1474560 | tf_op jit(solution)/shard_map/all_gather | solution.py:87
  7.9 215.0 %all-gather.8.cloned.1.call-start = ((), (), s32[]{:S(2)}) async-start(), calls=%async_computation.11 | async-start | bytes 1474560 | tf_op jit(solution)/shard_map/all_gather | solution.py:88
  8.7 219.4 %all-gather.10.cloned.1.call-start = ((), (), s32[]{:S(2)}) async-start(), calls=%async_computation.12 | async-start | bytes 1474560 | tf_op jit(solution)/shard_map/all_gather | solution.py:86
  9.4 275.8 %all-gather.14.cloned.1.call-start = ((), (), s32[]{:S(2)}) async-start(), calls=%async_computation.14 | async-start | bytes 1474560 | tf_op jit(solution)/shard_map/all_gather | solution.py:89
  10.0 560.1 %all-gather.16.cloned.1.call-start = ((), (), s32[]{:S(2)}) async-start(), calls=%async_computation.15 | async-start | bytes 11796480 | tf_op jit(solution)/shard_map/all_gather | solution.py:163
  20.5 15.2 %copy-start.90 = (bf16[8,12]{1,0:T(8,128)(2,1)S(1)}, bf16[8,12]{1,0:T(8,128)(2,1)}, u32[]{:S(2)}) copy-start(bf16[8,12]{1,0:T(8,128)(2,1)} %param.35) | copy-start | bytes 580
  20.5 20.6 %copy-start.89 = (bf16[192,8]{0,1:T(8,128)(2,1)S(1)}, bf16[192,8]{0,1:T(8,128)(2,1)}, u32[]{:S(2)}) copy-start(bf16[192,8]{0,1:T(8,128)(2,1)} %param.32) | copy-start | bytes 9220
  35.0 193.0 %copy-start.77 = (f32[768]{0:T(1024)}, f32[768]{0:T(1024)S(1)}, u32[]{:S(2)}) copy-start(f32[768]{0:T(1024)S(1)} %convert_element_type.671) | copy-start | bytes 9220
  57.2 26.4 %copy-start.83 = (s32[2048,1]{0,1:T(1,128)}, s32[2048,1]{0,1:T(1,128)S(1)}, u32[]{:S(2)}) copy-start(s32[2048,1]{0,1:T(1,128)S(1)} %compare_select_fusion) | copy-start | bytes 24580
  93.1 13.5 copy-start.5
  152.7 12.9 copy-start.27
  169.5 17.3 %copy-start.19 = (s32[524288]{0:T(1024)}, s32[524288]{0:T(1024)S(1)}, u32[]{:S(2)}) copy-start(s32[524288]{0:T(1024)S(1)} %add_add_fusion.3) | copy-start | bytes 6291460
  186.8 32.1 %copy-start.11 = (bf16[1024,768]{0,1:T(8,128)(2,1)S(1)}, bf16[1024,768]{0,1:T(8,128)(2,1)}, u32[]{:S(2)}) copy-start(bf16[1024,768]{0,1:T(8,128)(2,1)} %copy-done.10) | copy-start | bytes 4718596
  186.8 32.1 %copy-start.79 = (f32[1024]{0:T(1024)S(1)}, f32[1024]{0:T(1024)}, u32[]{:S(2)}) copy-start(f32[1024]{0:T(1024)} %fusion.127) | copy-start | bytes 12292
  292.4 13.4 copy-start.57
  312.5 17.0 %copy-start = (bf16[1024,768]{1,0:T(8,128)(2,1)S(1)}, bf16[1024,768]{1,0:T(8,128)(2,1)}, u32[]{:S(2)}) copy-start(bf16[1024,768]{1,0:T(8,128)(2,1)} %copy.231) | copy-start | bytes 4718596
  312.5 17.0 %copy-start.75 = (s32[3072]{0:T(1024)S(1)}, s32[3072]{0:T(1024)}, u32[]{:S(2)}) copy-start(s32[3072]{0:T(1024)} %get-tuple-element.194) | copy-start | bytes 36868
  329.5 13.6 copy-start.85
  456.4 108.9 %all-to-all-start = ((bf16[4,2,384,768]{3,2,1,0:T(8,128)(2,1)}), bf16[4,2,384,768]{3,2,1,0:T(8,128)(2,1)}, u32[]{:S(2)}, u32[]{:S(2)}) async-start(bf16[4,2,384,768]{3,2,1,0:T(8,128)(2,1)} %get-tuple-element.196), calls=%async_computation | async-start | bytes 9437184 | tf_op jit(solution)/shard_map/all_to_all | solution.py:154
  461.3 262.3 %all-gather.18.cloned.1.call-start = ((), (), s32[]{:S(2)}) async-start(), calls=%async_computation.16 | async-start | bytes 11796480 | tf_op jit(solution)/shard_map/all_gather | solution.py:164
  461.9 760.8 %reduce-scatter.20.cloned.1.call-start = ((), (), s32[]{:S(2)}) async-start(), calls=%async_computation.22 | async-start | bytes 11796480 | tf_op jit(solution)/shard_map/reduce_scatter | solution.py:241
  613.0 89.7 %copy-start.35 = (bf16[1,2,4,384,768]{4,3,2,1,0:T(8,128)(2,1)S(1)}, bf16[1,2,4,384,768]{4,3,2,1,0:T(8,128)(2,1)}, u32[]{:S(2)}) copy-start(bf16[1,2,4,384,768]{4,3,2,1,0:T(8,128)(2,1)} %copy.238) | copy-start | bytes 14155780
  805.3 108.9 %all-to-all-start.3 = ((bf16[2,4,384,768]{3,2,0,1:T(8,128)(2,1)}), bf16[2,4,384,768]{3,2,0,1:T(8,128)(2,1)}, u32[]{:S(2)}, u32[]{:S(2)}) async-start(bf16[2,4,384,768]{3,2,0,1:T(8,128)(2,1)} %copy.239), calls=%async_computation.3 | async-start | bytes 9437184 | tf_op jit(solution)/shard_map/all_to_all | solution.py:249
  810.3 412.5 %reduce-scatter.18.cloned.1.call-start = ((), (), s32[]{:S(2)}) async-start(), calls=%async_computation.21 | async-start | bytes 11796480 | tf_op jit(solution)/shard_map/reduce_scatter | solution.py:238
  872.8 46.5 %copy-start.84 = (s32[2048,1]{0,1:T(1,128)S(1)}, s32[2048,1]{0,1:T(1,128)}, u32[]{:S(2)}) copy-start(s32[2048,1]{0,1:T(1,128)} %copy-done.83) | copy-start | bytes 24580
  872.8 46.5 %copy-start.54 = (f32[12,512]{1,0:T(8,128)S(1)}, f32[12,512]{1,0:T(8,128)}, u32[]{:S(2)}) copy-start(f32[12,512]{1,0:T(8,128)} %copy-done.53) | copy-start | bytes 73732
  872.8 46.5 %copy-start.62 = (f32[12,512]{1,0:T(8,128)S(1)}, f32[12,512]{1,0:T(8,128)}, u32[]{:S(2)}) copy-start(f32[12,512]{1,0:T(8,128)} %copy-done.61) | copy-start | bytes 73732
  872.8 46.5 %copy-start.56 = (f32[12,512]{1,0:T(8,128)S(1)}, f32[12,512]{1,0:T(8,128)}, u32[]{:S(2)}) copy-start(f32[12,512]{1,0:T(8,128)} %copy-done.55) | copy-start | bytes 73732
  872.8 46.5 %copy-start.64 = (f32[12,512]{1,0:T(8,128)S(1)}, f32[12,512]{1,0:T(8,128)}, u32[]{:S(2)}) copy-start(f32[12,512]{1,0:T(8,128)} %copy-done.63) | copy-start | bytes 73732
  914.2 108.9 %all-to-all-start.1 = ((bf16[2,4,384,768]{3,2,0,1:T(8,128)(2,1)}), bf16[2,4,384,768]{3,2,0,1:T(8,128)(2,1)}, u32[]{:S(2)}, u32[]{:S(2)}) async-start(bf16[2,4,384,768]{3,2,0,1:T(8,128)(2,1)} %copy.233), calls=%async_computation.1 | async-start | bytes 9437184 | tf_op jit(solution)/shard_map/all_to_all | solution.py:178
  919.2 379.3 %reduce-scatter.22.cloned.1.call-start = ((), (), s32[]{:S(2)}) async-start(), calls=%async_computation.23 | async-start | bytes 245760
  1044.2 18.6 %copy-start.60 = (f32[1024,2]{0,1:T(2,128)S(1)}, f32[1024,2]{0,1:T(2,128)}, u32[]{:S(2)}) copy-start(f32[1024,2]{0,1:T(2,128)} %copy-done.59) | copy-start | bytes 24580
  1044.2 18.6 %copy-start.68 = (f32[1024]{0:T(1024)S(1)}, f32[1024]{0:T(1024)}, u32[]{:S(2)}) copy-start(f32[1024]{0:T(1024)} %copy-done.67) | copy-start | bytes 12292
  1044.2 18.6 %copy-start.70 = (f32[1024]{0:T(1024)S(1)}, f32[1024]{0:T(1024)}, u32[]{:S(2)}) copy-start(f32[1024]{0:T(1024)} %copy-done.69) | copy-start | bytes 12292
  1044.2 18.7 %copy-start.58 = (s32[1024,2]{0,1:T(2,128)S(1)}, s32[1024,2]{0,1:T(2,128)}, u32[]{:S(2)}) copy-start(s32[1024,2]{0,1:T(2,128)} %param.26) | copy-start | bytes 24580
  1084.0 12.2 copy-start.12
  1098.7 200.7 %reduce-scatter.16.cloned.1.call-start = ((), (), s32[]{:S(2)}) async-start(), calls=%async_computation.20 | async-start | bytes 1474560 | tf_op jit(solution)/shard_map/reduce_scatter | solution.py:350
  1103.6 195.8 %reduce-scatter.14.cloned.1.call-start = ((), (), s32[]{:S(2)}) async-start(), calls=%async_computation.19 | async-start | bytes 1474560 | tf_op jit(solution)/shard_map/reduce_scatter | solution.py:347
  1130.9 168.5 %reduce-scatter.12.cloned.1.call-start = ((), (), s32[]{:S(2)}) async-start(), calls=%async_computation.18 | async-start | bytes 1474560 | tf_op jit(solution)/shard_map/reduce_scatter | solution.py:344
  1130.9 18.6 %slice-start.3 = ((s8[12582912]{0:T(1024)(128)(4,1)}), s8[4194304]{0:T(1024)(128)(4,1)S(1)}, s32[]{:S(2)}) async-start(s8[12582912]{0:T(1024)(128)(4,1)} %bitcast.185), calls=%async_computation.28 | async-start | bytes 8388608
  1130.9 18.7 %slice-start.4 = ((s8[12582912]{0:T(1024)(128)(4,1)}), s8[4194304]{0:T(1024)(128)(4,1)S(1)}, s32[]{:S(2)}) async-start(s8[12582912]{0:T(1024)(128)(4,1)} %bitcast.185), calls=%async_computation.29 | async-start | bytes 8388608
  1131.0 20.5 %slice-start.5 = ((s8[12582912]{0:T(1024)(128)(4,1)}), s8[4194304]{0:T(1024)(128)(4,1)S(1)}, s32[]{:S(2)}) async-start(s8[12582912]{0:T(1024)(128)(4,1)} %bitcast.185), calls=%async_computation.30 | async-start | bytes 8388608
  1149.6 19.3 %copy-start.2 = (bf16[12,512,1024]{2,1,0:T(8,128)(2,1)}, bf16[12,512,1024]{2,1,0:T(8,128)(2,1)S(1)}, u32[]{:S(2)}) copy-start(bf16[12,512,1024]{2,1,0:T(8,128)(2,1)S(1)} %multiply_convert_fusion.1) | copy-start | bytes 37748740
  1151.5 12.5 copy-start.29
  1174.9 124.5 %reduce-scatter.10.cloned.1.call-start = ((), (), s32[]{:S(2)}) async-start(), calls=%async_computation.17 | async-start | bytes 1474560 | tf_op jit(solution)/shard_map/reduce_scatter | solution.py:341
  1192.6 211.8 %all-reduce.14.cloned.1.call-start = ((), (), s32[]{:S(2)}) async-start(), calls=%async_computation.24 | async-start | bytes 9437184 | tf_op jit(solution)/shard_map/psum | solution.py:246
  1240.3 29.2 %copy-start.20 = (s32[524288]{0:T(1024)S(1)}, s32[524288]{0:T(1024)}, u32[]{:S(2)}) copy-start(s32[524288]{0:T(1024)} %copy-done.19) | copy-start | bytes 6291460
  1240.3 39.2 %slice-start.6 = ((s8[8388608]{0:T(1024)(128)(4,1)}), s8[4194304]{0:T(1024)(128)(4,1)S(1)}, s32[]{:S(2)}) async-start(s8[8388608]{0:T(1024)(128)(4,1)} %bitcast.203), calls=%async_computation.31 | async-start | bytes 8388608
  (77 other events, 397.8 us)
Sparse Core Ops, SparseCore 0:
  9.8 29.8 all-gather.11
  41.6 27.7 all-gather.7
  71.3 27.7 all-gather.9
  100.8 27.7 all-gather.13
  130.2 96.3 all-gather.15
  463.7 99.7 all-gather.17
  723.7 94.7 reduce-scatter.19
  832.2 97.9 reduce-scatter.17
  1098.8 23.6 reduce-scatter.21
  1125.2 28.9 reduce-scatter.15
  1157.2 28.5 reduce-scatter.13
  1188.6 28.4 reduce-scatter.11
  1220.0 28.5 reduce-scatter.9
  1251.0 29.5 all-reduce.13
where the time goes:
time: 1430 us; the launch traced here: 1420 us
  matrix products  382 us (27%)
  local copies, waits for them, and re-layouts  335 us (23%)
  blocking collectives  245 us (17%)
  waiting for transfers between devices  218 us (15%)
  other arithmetic  205 us (14%)
  between operations  17.5 us (1%)
  starting transfers between devices  15.5 us (1%)
    unnamed x245, local copies, waits for them, and re-layouts  155 us
    all_to_all x1, blocking collectives, local(): lax.all_to_all(grad_send.reshape(groups, local_experts, capacity, model_w...  106 us
    psum x1, blocking collectives, local(): lax.psum((dense_shares[0], dense_shares[1], dense_shares[2], dense_shares...  105 us
    all_to_all x1, waiting for transfers between devices, local(): lax.all_to_all(send_rows.reshape(groups, local_experts, capacity, model_w...  98.5 us
    convert_element_type x1, other arithmetic, local(): hidden_bf = gelu_exact(pre_act).astype(jnp.bfloat16)  89.6 us
    all_to_all x1, waiting for transfers between devices, local(): lax.all_to_all(expert_out.reshape(local_experts, groups, capacity, model_...  74.6 us
    dot_general x1, matrix products, local(): jnp.einsum('erd,edf->erf', expert_in, up_full, preferred_element_type=jnp...  42.9 us
    dot_general x1, matrix products, local(): jnp.einsum('erd,efd->erf', grad_expert_out, down_full, preferred_element_...  42 us
  transfers between devices with their start and end apart: 17, of which 3 were waited for; matrix products, arithmetic and copies ran while one was open for 63% of the time, Pallas kernels for 0%

commit v1 on v0

v1 whole, which is shorter than its diff:
```python
import jax
import jax.numpy as jnp
from jax import lax
from jax.experimental import pallas as pl
from jax.experimental.pallas import tpu as pltpu
from jax.sharding import PartitionSpec as P

distance_edges = (18, 21, 24, 27, 31, 35, 40, 45, 51, 58, 66, 75, 85, 97, 110)


def bucket_ids(distance):
    distance = jnp.maximum(distance, 0)
    result = jnp.minimum(distance, 16)
    for edge_value in distance_edges:
        result = result + (distance >= edge_value).astype(jnp.int32)
    return result


def dot_f32(left, right, left_dim, right_dim):
    return lax.dot_general(
        left, right, (((left_dim,), (right_dim,)), ((), ())), preferred_element_type=jnp.float32
    )


TILE = 128
QUERY_ROWS = 256
HEAD_DIM = 64


def key_segments(begin):
    near_begin = max(begin - TILE, 0)
    parts = [(near_begin, begin + QUERY_ROWS, near_begin - (begin - TILE))]
    if near_begin > 0:
        parts.append((0, near_begin, None))
    return parts


def attend_kernel(q_ref, k_ref, v_ref, window_ref, out_ref, lse_ref):
    scale = HEAD_DIM ** (-0.5)
    for head in range(2):
        cols = slice(head * HEAD_DIM, (head + 1) * HEAD_DIM)
        for begin in range(0, q_ref.shape[0], QUERY_ROWS):
            rows = slice(begin, begin + QUERY_ROWS)
            query = (q_ref[rows, cols].astype(jnp.float32) * scale).astype(jnp.bfloat16)
            parts = key_segments(begin)
            scores = []
            for low, high, window_row in parts:
                score = dot_f32(k_ref[low:high, cols], query, 1, 1)
                if window_row is not None:
                    score = score + window_ref[head, window_row:, :]
                scores.append(score)
            row_max = jnp.max(scores[0], axis=0, keepdims=True)
            for score in scores[1:]:
                row_max = jnp.maximum(row_max, jnp.max(score, axis=0, keepdims=True))
            total = jnp.zeros((1, QUERY_ROWS), jnp.float32)
            acc = jnp.zeros((HEAD_DIM, QUERY_ROWS), jnp.float32)
            for (low, high, window_row), score in zip(parts, scores):
                prob = jnp.exp(score - row_max)
                total = total + jnp.sum(prob, axis=0, keepdims=True)
                acc = acc + dot_f32(v_ref[low:high, cols], prob.astype(jnp.bfloat16), 0, 0)
            out_ref[rows, cols] = (acc / total).T.astype(jnp.bfloat16)
            lse_ref[0, head : head + 1, rows] = row_max + jnp.log(total)


def attend_grad_kernel(
    q_ref, k_ref, v_ref, go_ref, window_ref, lse_ref, dq_ref, dk_ref, dv_ref, tile_ref, dk_acc, dv_acc
):
    scale = HEAD_DIM ** (-0.5)
    first = slice(0, TILE)
    second = slice(TILE, 2 * TILE)
    for head in range(2):
        cols = slice(head * HEAD_DIM, (head + 1) * HEAD_DIM)
        tile_ref[head] = jnp.zeros((3 * TILE, TILE), jnp.float32)
        last_begin = q_ref.shape[0] - QUERY_ROWS
        for begin in range(last_begin, -1, -QUERY_ROWS):
            rows = slice(begin, begin + QUERY_ROWS)
            query = (q_ref[rows, cols].astype(jnp.float32) * scale).astype(jnp.bfloat16)
            grad_out = go_ref[rows, cols]
            lse = lse_ref[0, head : head + 1, rows]
            parts = key_segments(begin)
            probs = []
            grad_probs = []
            delta = jnp.zeros((1, QUERY_ROWS), jnp.float32)
            for low, high, window_row in parts:
                score = dot_f32(k_ref[low:high, cols], query, 1, 1)
                if window_row is not None:
                    score = score + window_ref[head, window_row:, :]
                prob = jnp.exp(score - lse)
                grad_prob = dot_f32(v_ref[low:high, cols], grad_out, 1, 1)
                delta = delta + jnp.sum(prob * grad_prob, axis=0, keepdims=True)
                probs.append(prob)
                grad_probs.append(grad_prob)
            grad_query = jnp.zeros((HEAD_DIM, QUERY_ROWS), jnp.float32)
            far_sum = jnp.zeros((TILE, TILE), jnp.float32)
            for (low, high, window_row), prob, grad_prob in zip(parts, probs, grad_probs):
                grad_score = prob * (grad_prob - delta)
                grad_bf = grad_score.astype(jnp.bfloat16)
                value_term = dot_f32(prob.astype(jnp.bfloat16), grad_out, 1, 0)
                key_term = dot_f32(grad_bf, query, 1, 0)
                if begin == last_begin:
                    dv_acc[low:high, :] = value_term
                    dk_acc[low:high, :] = key_term
                else:
                    dv_acc[low:high, :] += value_term
                    dk_acc[low:high, :] += key_term
                grad_query = grad_query + dot_f32(k_ref[low:high, cols], grad_bf, 0, 0)
                if window_row is None:
                    for chunk in range(0, high - low, TILE):
                        piece = grad_score[chunk : chunk + TILE]
                        far_sum = far_sum + piece[:, first] + piece[:, second]
                else:
                    at = TILE - window_row
                    if window_row == 0:
                        tile_ref[head, 0:TILE, :] += grad_score[0:TILE, first]
                        far_sum = far_sum + grad_score[0:TILE, second]
                    tile_ref[head, 0:TILE, :] += grad_score[at : at + TILE, second]
                    tile_ref[head, TILE : 2 * TILE, :] += (
                        grad_score[at : at + TILE, first]
                        + grad_score[at + TILE : at + 2 * TILE, second]
                    )
            tile_ref[head, 2 * TILE :, :] += far_sum
            dq_ref[rows, cols] = (grad_query * scale).T.astype(jnp.bfloat16)
        dk_ref[:, cols] = dk_acc[...].astype(jnp.bfloat16)
        dv_ref[:, cols] = dv_acc[...].astype(jnp.bfloat16)


def attend(qkv, window):
    seq_len, width = qkv.shape[0], qkv.shape[1] // 3
    pairs = width // (2 * HEAD_DIM)
    wide = (seq_len, 2 * HEAD_DIM)
    return pl.pallas_call(
        attend_kernel,
        grid=(pairs,),
        in_specs=[
            pl.BlockSpec(wide, lambda p: (0, p)),
            pl.BlockSpec(wide, lambda p: (0, p + pairs)),
            pl.BlockSpec(wide, lambda p: (0, p + 2 * pairs)),
            pl.BlockSpec((2,) + window.shape[1:], lambda p: (p, 0, 0)),
        ],
        out_specs=[
            pl.BlockSpec(wide, lambda p: (0, p)),
            pl.BlockSpec((1, 2, seq_len), lambda p: (p, 0, 0)),
        ],
        out_shape=[
            jax.ShapeDtypeStruct((seq_len, width), jnp.bfloat16),
            jax.ShapeDtypeStruct((pairs, 2, seq_len), jnp.float32),
        ],
        compiler_params=pltpu.CompilerParams(vmem_limit_bytes=48 * 1024 * 1024),
    )(qkv, qkv, qkv, window)


def attend_grad(qkv, grad_heads, window, lse):
    seq_len, width = grad_heads.shape
    pairs = width // (2 * HEAD_DIM)
    wide = (seq_len, 2 * HEAD_DIM)
    grad_shape = jax.ShapeDtypeStruct((seq_len, width), jnp.bfloat16)
    return pl.pallas_call(
        attend_grad_kernel,
        grid=(pairs,),
        in_specs=[
            pl.BlockSpec(wide, lambda p: (0, p)),
            pl.BlockSpec(wide, lambda p: (0, p + pairs)),
            pl.BlockSpec(wide, lambda p: (0, p + 2 * pairs)),
            pl.BlockSpec(wide, lambda p: (0, p)),
            pl.BlockSpec((2,) + window.shape[1:], lambda p: (p, 0, 0)),
            pl.BlockSpec((1, 2, seq_len), lambda p: (p, 0, 0)),
        ],
        out_specs=[
            pl.BlockSpec(wide, lambda p: (0, p)),
            pl.BlockSpec(wide, lambda p: (0, p)),
            pl.BlockSpec(wide, lambda p: (0, p)),
            pl.BlockSpec((2, 3 * TILE, TILE), lambda p: (p, 0, 0)),
        ],
        out_shape=[
            grad_shape,
            grad_shape,
            grad_shape,
            jax.ShapeDtypeStruct((2 * pairs, 3 * TILE, TILE), jnp.float32),
        ],
        scratch_shapes=[
            pltpu.VMEM((seq_len, HEAD_DIM), jnp.float32),
            pltpu.VMEM((seq_len, HEAD_DIM), jnp.float32),
        ],
        compiler_params=pltpu.CompilerParams(vmem_limit_bytes=48 * 1024 * 1024),
    )(qkv, qkv, qkv, grad_heads, window, lse)


def up_kernel(rows_ref, up_ref, hidden_ref, slope_ref):
    pre = dot_f32(rows_ref[0], up_ref[0], 1, 0)
    bell = jnp.exp(pre * pre * -0.5)
    inv = 1.0 / (1.0 + 0.23164189 * jnp.abs(pre))
    series = inv * (
        0.127414796
        + inv * (-0.142248368 + inv * (0.7107068705 + inv * (-0.7265760135 + inv * 0.5307027145)))
    )
    tail = series * bell
    cdf = jnp.where(pre >= 0, 1.0 - tail, tail)
    hidden_ref[0] = (pre * cdf).astype(jnp.bfloat16)
    slope_ref[0] = (cdf + pre * bell * 0.3989422804).astype(jnp.bfloat16)


def up_project(rows_in, up_full):
    experts, row_count, width = rows_in.shape
    hidden_width = up_full.shape[2]
    row_block = 512 if row_count % 512 == 0 else row_count
    col_block = 512
    shape = jax.ShapeDtypeStruct((experts, row_count, hidden_width), jnp.bfloat16)
    out_spec = pl.BlockSpec((1, row_block, col_block), lambda e, f, r: (e, r, f))
    return pl.pallas_call(
        up_kernel,
        grid=(experts, hidden_width // col_block, row_count // row_block),
        in_specs=[
            pl.BlockSpec((1, row_block, width), lambda e, f, r: (e, r, 0)),
            pl.BlockSpec((1, width, col_block), lambda e, f, r: (e, 0, f)),
        ],
        out_specs=[out_spec, out_spec],
        out_shape=[shape, shape],
        compiler_params=pltpu.CompilerParams(vmem_limit_bytes=48 * 1024 * 1024),
    )(rows_in, up_full)


def inv_rms(values):
    return lax.rsqrt(jnp.mean(values * values, axis=-1, keepdims=True) + 1e-06)


def rms_pull(values, inv, gain_vec, grad):
    normed = values * inv
    scaled = grad * gain_vec
    grad_in = inv * (scaled - normed * jnp.mean(scaled * normed, axis=-1, keepdims=True))
    return grad_in, jnp.sum(grad * normed, axis=0)


def to_experts(slots, groups):
    shape = slots.shape
    sent = slots.reshape((groups, shape[0] // groups) + shape[1:])
    got = lax.all_to_all(sent, "expert", split_axis=0, concat_axis=2, tiled=True)
    return got.reshape((got.shape[1],) + got.shape[2:])


def to_tokens(slots, groups):
    shape = slots.shape
    sent = slots.reshape((shape[0], groups, shape[1] // groups) + shape[2:])
    got = lax.all_to_all(sent, "expert", split_axis=1, concat_axis=0, tiled=True)
    return got.reshape((got.shape[0],) + got.shape[2:])


def local(
    tokens,
    routes,
    cotangent,
    w_query,
    w_key,
    w_value,
    w_out,
    w_router,
    gain_attn,
    gain_moe,
    bias_table,
    expert_up,
    expert_down,
):
    seq_len, width = tokens.shape
    head_count = bias_table.shape[1]
    local_experts = expert_up.shape[0]
    groups = lax.axis_size("expert")
    quarters = lax.axis_size("dp")
    expert_count = groups * local_experts
    top_count = routes.shape[1]
    capacity = 3 * seq_len * top_count // (2 * expert_count)
    share = w_query.shape[0]
    bias_size = bias_table.size
    small = jnp.concatenate(
        [
            w_router,
            gain_attn[:, None],
            gain_moe[:, None],
            jnp.pad(bias_table.reshape(-1), (0, share - bias_size))[:, None],
        ],
        axis=1,
    )
    small = jnp.pad(small, ((0, 0), (0, -small.shape[1] % TILE)))
    dense = lax.all_gather(
        jnp.concatenate([w_query, w_key, w_value, w_out, small], axis=1), "dp", axis=0, tiled=True
    )
    up_full = lax.all_gather(expert_up, "dp", axis=2, tiled=True)
    down_full = lax.all_gather(expert_down, "dp", axis=1, tiled=True)
    expert_range = jnp.arange(expert_count, dtype=jnp.int32)
    chosen = routes.T[:, None, :] == expert_range[None, :, None]
    match = jnp.any(chosen, axis=0)
    row_range = jnp.arange(seq_len, dtype=jnp.int32)
    before = (row_range[:, None] < row_range[None, :]).astype(jnp.bfloat16)
    position = dot_f32(match.astype(jnp.bfloat16), before, 1, 0).astype(jnp.int32)
    position = jnp.where(match, position, -1)
    slot_range = jnp.arange(capacity, dtype=jnp.int32)
    place = (position[:, None, :] == slot_range[None, :, None]).astype(jnp.bfloat16)
    place_flat = place.reshape(expert_count * capacity, seq_len)

    def dispatch(rows):
        slots = dot_f32(place_flat, rows, 1, 0).astype(jnp.bfloat16)
        return slots.reshape(expert_count, capacity, width)

    cot_in = to_experts(dispatch(cotangent), groups)

    inputs = tokens.astype(jnp.float32)
    inv_one = inv_rms(inputs)
    qkv_w = dense[:, : 3 * width]
    out_w = dense[:, 3 * width : 4 * width]
    small_full = dense[:, 4 * width :]
    router_full = small_full[:, :expert_count]
    gain_one = small_full[:, expert_count].astype(jnp.float32)
    gain_two = small_full[:, expert_count + 1].astype(jnp.float32)
    table = small_full[:, expert_count + 2].reshape(quarters, share)[:, :bias_size]
    table = table.reshape(-1, head_count)
    buckets = table.shape[0]

    near_keys = jnp.arange(-TILE, TILE, dtype=jnp.int32)
    distance = jnp.arange(TILE, dtype=jnp.int32)[None, :] - near_keys[:, None]
    bucket_range = jnp.arange(buckets, dtype=jnp.int32)
    one_hot = bucket_ids(distance)[None] == bucket_range[:, None, None]
    near = jnp.einsum(
        "kh,krc->hrc", table, one_hot.astype(jnp.bfloat16), preferred_element_type=jnp.float32
    ) - table[-1].astype(jnp.float32)[:, None, None]
    near = jnp.where(distance[None] >= 0, near, -1e30)
    beside, diagonal = near[:, :TILE], near[:, TILE:]
    window = jnp.concatenate(
        [
            jnp.concatenate([beside, jnp.zeros_like(beside)], axis=2),
            jnp.concatenate([diagonal, beside], axis=2),
            jnp.concatenate([jnp.full_like(diagonal, -1e30), diagonal], axis=2),
        ],
        axis=1,
    )

    norm_one_bf = (inputs * inv_one * gain_one).astype(jnp.bfloat16)
    qkv = dot_f32(norm_one_bf, qkv_w, 1, 0).astype(jnp.bfloat16)
    attn_bf, lse = attend(qkv, window)
    middle = inputs + dot_f32(attn_bf, out_w, 1, 0)
    inv_two = inv_rms(middle)
    norm_two_bf = (middle * inv_two * gain_two).astype(jnp.bfloat16)
    expert_in = to_experts(dispatch(norm_two_bf), groups)

    logits = dot_f32(router_full, norm_two_bf, 0, 1)
    picked = jnp.sum(jnp.where(chosen, logits[None], 0.0), axis=1)
    gates = jax.nn.softmax(picked, axis=0)
    gate_of = jnp.sum(jnp.where(chosen, gates[:, None, :], 0.0), axis=0)
    gate_slots = jnp.sum(place.astype(jnp.float32) * gate_of[:, None, :], axis=2)
    gate_in = to_experts(gate_slots, groups)

    hidden_bf, slope_bf = up_project(expert_in, up_full)
    expert_out = jnp.einsum(
        "erf,efd->erd", hidden_bf, down_full, preferred_element_type=jnp.float32
    ).astype(jnp.bfloat16)
    cot_f32 = cot_in.astype(jnp.float32)
    grad_gate_slots = to_tokens(jnp.sum(expert_out.astype(jnp.float32) * cot_f32, axis=2), groups)
    grad_expert_out = (cot_f32 * gate_in[:, :, None]).astype(jnp.bfloat16)
    grad_hidden = jnp.einsum(
        "erd,efd->erf", grad_expert_out, down_full, preferred_element_type=jnp.float32
    )
    grad_pre = (grad_hidden * slope_bf.astype(jnp.float32)).astype(jnp.bfloat16)
    grad_expert_in = jnp.einsum(
        "erf,edf->erd", grad_pre, up_full, preferred_element_type=jnp.float32
    ).astype(jnp.bfloat16)
    grad_back = to_tokens(grad_expert_in, groups)
    grad_down = jnp.einsum(
        "erf,erd->efd", hidden_bf, grad_expert_out, preferred_element_type=jnp.float32
    ).astype(jnp.bfloat16)
    grad_up = jnp.einsum(
        "erd,erf->edf", expert_in, grad_pre, preferred_element_type=jnp.float32
    ).astype(jnp.bfloat16)
    grad_down = lax.psum(lax.psum_scatter(grad_down, "dp", scatter_dimension=1, tiled=True), "rep")
    grad_up = lax.psum(lax.psum_scatter(grad_up, "dp", scatter_dimension=2, tiled=True), "rep")

    expert_out, grad_back = lax.optimization_barrier((expert_out, grad_back))
    returned = to_tokens(expert_out, groups).reshape(expert_count * capacity, width)
    place_gate = (place * gate_of.astype(jnp.bfloat16)[:, None, :]).reshape(place_flat.shape)
    output = (middle + dot_f32(place_gate, returned, 0, 0)).astype(jnp.bfloat16)

    grad_output = cotangent.astype(jnp.float32)
    sign = chosen[0].astype(jnp.float32) - chosen[1].astype(jnp.float32)
    grad_gap = jnp.sum(
        sign * jnp.sum(place.astype(jnp.float32) * grad_gate_slots[:, :, None], axis=1), axis=0
    )
    grad_logits = (sign * (gates[0] * gates[1] * grad_gap)[None, :]).astype(jnp.bfloat16)
    grad_router = dot_f32(norm_two_bf, grad_logits, 0, 1)
    grad_norm_two = dot_f32(
        place_flat, grad_back.reshape(expert_count * capacity, width), 0, 0
    ) + dot_f32(grad_logits, router_full, 0, 1)
    grad_middle, grad_gain_two = rms_pull(middle, inv_two, gain_two, grad_norm_two)
    grad_middle = grad_output + grad_middle
    grad_attn_bf = grad_middle.astype(jnp.bfloat16)
    grad_out_w = dot_f32(attn_bf, grad_attn_bf, 0, 0)
    grad_heads = dot_f32(grad_attn_bf, out_w, 1, 1).astype(jnp.bfloat16)
    grad_q, grad_k, grad_v, tiles = attend_grad(qkv, grad_heads, window, lse)
    grad_qkv = jnp.concatenate([grad_q, grad_k, grad_v], axis=1)
    grad_qkv_w = dot_f32(norm_one_bf, grad_qkv, 0, 0)
    grad_norm_one = dot_f32(grad_qkv, qkv_w, 1, 1)
    grad_tokens, grad_gain_one = rms_pull(inputs, inv_one, gain_one, grad_norm_one)
    grad_tokens = grad_middle + grad_tokens
    grad_table = jnp.einsum(
        "hrc,krc->kh",
        tiles[:, : 2 * TILE],
        one_hot.astype(jnp.float32),
        precision=lax.Precision.HIGHEST,
    )
    far_total = jnp.sum(tiles[:, 2 * TILE :], axis=(1, 2))
    grad_table = grad_table + jnp.where(
        bucket_range[:, None] == buckets - 1, far_total[None, :], 0.0
    )
    table_column = jnp.pad(
        grad_table.reshape(quarters, bias_size), ((0, 0), (0, share - bias_size))
    ).reshape(-1, 1)
    small_grad = jnp.concatenate(
        [grad_router, grad_gain_one[:, None], grad_gain_two[:, None], table_column], axis=1
    )
    small_grad = jnp.pad(small_grad, ((0, 0), (0, small.shape[1] - small_grad.shape[1])))
    dense_grad = jnp.concatenate(
        [
            grad_qkv_w.astype(jnp.bfloat16),
            grad_out_w.astype(jnp.bfloat16),
            small_grad.astype(jnp.bfloat16),
        ],
        axis=1,
    )
    dense_grad = lax.psum_scatter(dense_grad, "dp", scatter_dimension=0, tiled=True)
    dense_grad = lax.psum(dense_grad, ("rep", "expert")).astype(jnp.float32)
    small_sum = dense_grad[:, 4 * width :]
    return (
        output,
        grad_tokens,
        dense_grad[:, :width],
        dense_grad[:, width : 2 * width],
        dense_grad[:, 2 * width : 3 * width],
        dense_grad[:, 3 * width : 4 * width],
        small_sum[:, :expert_count],
        small_sum[:, expert_count],
        small_sum[:, expert_count + 1],
        small_sum[:bias_size, expert_count + 2].reshape(bias_table.shape),
        grad_up.astype(jnp.float32),
        grad_down.astype(jnp.float32),
    )


def solution(mesh):
    placed = (
        P(("rep", "dp", "expert"), None),
        P(("rep", "dp", "expert"), None),
        P(("rep", "dp", "expert"), None),
        P("dp", None),
        P("dp", None),
        P("dp", None),
        P("dp", None),
        P("dp", None),
        P("dp"),
        P("dp"),
        P("dp", None),
        P("expert", None, "dp"),
        P("expert", "dp", None),
    )
    return jax.shard_map(
        local,
        mesh=mesh,
        in_specs=placed,
        out_specs=(
            P(("rep", "dp", "expert"), None),
            P(("rep", "dp", "expert"), None),
            P("dp", None),
            P("dp", None),
            P("dp", None),
            P("dp", None),
            P("dp", None),
            P("dp"),
            P("dp"),
            P("dp", None),
            P("expert", None, "dp"),
            P("expert", "dp", None),
        ),
        check_vma=False,
    )
```

time: 1430 us -> 965 us (0.67)
  waiting for transfers between devices: 218 us -> 464 us
  blocking collectives: 245 us -> 6.95 us
  local copies, waits for them, and re-layouts: 335 us -> 110 us
  matrix products: 382 us -> 184 us
  other arithmetic: 205 us -> 41.9 us
  Pallas kernels: 0 us -> 111 us
    dot_general x40 -> x18, matrix products: 297 us -> 112 us  [the longest x14 62.6 us: dot_f32(): lax.dot_general(left, right, (((left_dim,), (right_dim,)), ((), ())), pre...]
    reduce_scatter x6 -> x3, waiting for transfers between devices: 0.07 us -> 184 us  [the longest x1 98 us: local(): lax.psum_scatter(grad_up, 'dp', scatter_dimension=2, tiled=True)]
    unnamed x245 -> x103, local copies, waits for them, and re-layouts: 155 us -> 30.7 us
    convert_element_type x12 -> x8, other arithmetic: 134 us -> 16.7 us  [the longest x1 6.62 us: local(): cot_f32 = cot_in.astype(jnp.float32)]
    pallas_call x0 -> x3, Pallas kernels: none -> 111 us  [the longest x1 52.5 us: up_project(): pl.pallas_call(up_kernel, grid=(experts, hidden_width // col_block, row_c...]
    psum x1 -> x0, blocking collectives: 105 us -> none  [local(): lax.psum((dense_shares[0], dense_shares[1], dense_shares[2], dense_shares...]
    all_to_all x1, blocking collectives: 106 us -> 6.95 us  [to_experts(): lax.all_to_all(sent, 'expert', split_axis=0, concat_axis=2, tiled=True)]
    gather x9 -> x0, local copies, waits for them, and re-layouts: 71.8 us -> none  [the longest x1 17 us: local(): weighted[source_ids]]
  transfers between devices with their start and end apart: 17 -> 13, of which waited for: 3 -> 9; matrix products, arithmetic and copies ran while one was open for 63% -> 20% of each run, Pallas kernels for 0% -> 8%
where the time goes in v1:
time: 965 us; the launch traced here: 958 us
  waiting for transfers between devices  464 us (48%)
  matrix products  184 us (19%)
  Pallas kernels  111 us (12%)
  local copies, waits for them, and re-layouts  110 us (11%)
  other arithmetic  41.9 us (4%)
  starting transfers between devices  24.4 us (3%)
  between operations  15.1 us (2%)
    all_to_all x3, waiting for transfers between devices, to_tokens(): lax.all_to_all(sent, 'expert', split_axis=1, concat_axis=0, tiled=True)  102 us
    reduce_scatter x1, waiting for transfers between devices, local(): lax.psum_scatter(grad_up, 'dp', scatter_dimension=2, tiled=True)  98 us
    all_to_all x2, waiting for transfers between devices, to_experts(): lax.all_to_all(sent, 'expert', split_axis=0, concat_axis=2, tiled=True)  88.2 us
    reduce_scatter x1, waiting for transfers between devices, local(): lax.psum_scatter(grad_down, 'dp', scatter_dimension=1, tiled=True)  85.9 us
    dot_general x14, matrix products, dot_f32(): lax.dot_general(left, right, (((left_dim,), (right_dim,)), ((), ())), pre...  62.6 us
    pallas_call x1, Pallas kernels, up_project(): pl.pallas_call(up_kernel, grid=(experts, hidden_width // col_block, row_c...  52.5 us
    psum x1, waiting for transfers between devices, local(): dense_grad = lax.psum(dense_grad, ('rep', 'expert')).astype(jnp.float32)  36.9 us
    pallas_call x1, Pallas kernels, attend_grad(): pl.pallas_call(attend_grad_kernel, grid=(pairs,), in_specs=[pl.BlockSpec(...  34.5 us
  transfers between devices with their start and end apart: 13, of which 9 were waited for; matrix products, arithmetic and copies ran while one was open for 20% of the time, Pallas kernels for 8%

profile of v1, /device:TPU:1, one launch (start us, length us, event | category | flops | bytes accessed | tf_op | source)
XLA Modules:
  0.0 957.8 jit_solution(3074255639975285517)
XLA Ops:
  18.8 6.7 convolution_convert_fusion.4
  25.5 6.8 copy.123
  32.3 5.5 all-to-all-start.1
  41.5 6.1 copy.119
  50.3 25.8 %all-gather.4.cloned.1.call-done = bf16[768,3200]{1,0:T(8,128)(2,1)} async-done(((bf16[192,3200]{1,0:T(8,128)(2,1)}), bf16[768,3200]{1,0:T(8,128)(2,1)}) %all-gather.4.cloned.1.call-update) | async-done | bytes 4915216 | tf_op jit(solution)/shard_map/all_gather | solution.py:282
  83.1 5.7 convolution_convert_fusion.2.q_ref.k_ref.v_ref
  88.8 24.1 %shard_map.220 = (bf16[1024,768]{1,0:T(8,128)(2,1)S(1)}, f32[6,2,1024]{2,1,0:T(2,128)S(1)}) custom-call(bf16[1024,2304]{1,0:T(8,128)(2,1)} %convolution_convert_fusion.2.q_ref.k_ref.v_ref, bf16[1024,2304]{1,0:T(8,128)(2,1)} %convolution_convert_fusion.2.q_ref.k_ref.v_ref, bf16[1024,2304]{1,0:T(8,128)(2,1)} %convolution_convert_fusion.2.q_ref.k_ref.v_ref, ...), custom_call_target="tpu_custom_call" | custom-call | tf_op jit(solution)/shard_map/pallas_call | solution.py:131
  117.6 6.7 convolution_convert_fusion.5
  124.3 17.7 %all-to-all-done.1 = bf16[4,2,384,768]{2,3,1,0:T(8,128)(2,1)} async-done(((bf16[4,2,384,768]{2,3,1,0:T(8,128)(2,1)}), bf16[4,2,384,768]{2,3,1,0:T(8,128)(2,1)}, u32[]{:S(2)}, u32[]{:S(2)}) %all-to-all-start.1) | async-done | bytes 4718624 | tf_op jit(solution)/shard_map/all_to_all | solution.py:236
  142.0 5.2 all-to-all-start
  147.2 6.6 convert_bitcast_fusion
  153.8 13.4 %copy.124 = f32[1,2,4,384,768]{3,2,4,1,0:T(4,128)} copy(f32[1,2,4,384,768]{3,4,1,2,0:T(8,128)} %convert_bitcast_fusion) | data formatting | bytes 18874368 | tf_op jit(solution)/shard_map/convert_element_type | solution.py:353
  167.2 12.0 %reshape.301 = f32[2,1536,768]{1,2,0:T(8,128)} reshape(f32[1,2,4,384,768]{3,2,4,1,0:T(4,128)} %copy.124) | data formatting | bytes 18874368 | tf_op jit(solution)/shard_map/convert_element_type | solution.py:353
  180.7 70.5 %all-to-all-done = bf16[4,2,384,768]{3,2,1,0:T(8,128)(2,1)} async-done(((bf16[4,2,384,768]{3,2,1,0:T(8,128)(2,1)}), bf16[4,2,384,768]{3,2,1,0:T(8,128)(2,1)}, u32[]{:S(2)}, u32[]{:S(2)}) %all-to-all-start) | async-done | bytes 4718624 | tf_op jit(solution)/shard_map/all_to_all | solution.py:236
  251.2 4.8 copy.121
  258.3 52.5 %shard_map.221 = (bf16[2,1536,3072]{2,1,0:T(8,128)(2,1)}, bf16[2,1536,3072]{2,1,0:T(8,128)(2,1)}) custom-call(bf16[2,1536,768]{2,1,0:T(8,128)(2,1)S(1)} %bitcast.93, bf16[2,768,3072]{2,1,0:T(8,128)(2,1)} %all-gather.6.cloned.1.call-done.up_ref), custom_call_target="tpu_custom_call" | custom-call | tf_op jit(solution)/shard_map/pallas_call | solution.py:209
  310.8 24.0 %multiply_reduce_fusion = (f32[2,1536]{1,0:T(2,128)}, bf16[2,1536,768]{1,2,0:T(8,128)(2,1)}) fusion(f32[2,1536,768]{1,2,0:T(8,128)} %reshape.301, bf16[2,1536,3072]{2,1,0:T(8,128)(2,1)} %get-tuple-element.23, bf16[2,3072,768]{1,2,0:T(8,128)(2,1)} %all-gather.8.cloned.1.call-done), kind=kOutput, calls=%fused_computation.13 | convolution fusion | flops 14504948736 | bytes 42479616 | tf_op jit(solution)/shard_map/erf,efd->erd/dot_general | solution.py:350
  334.8 3.3 all-to-all-start.5
  338.1 4.4 all-to-all-done.5
  342.5 3.6 fusion.1
  346.0 7.0 all_to_all.84
  353.0 25.8 %multiply_convert_fusion = bf16[2,1536,3072]{2,1,0:T(8,128)(2,1)} fusion(bf16[2,1536,3072]{2,1,0:T(8,128)(2,1)} %get-tuple-element.24, bf16[2,3072,768]{1,2,0:T(8,128)(2,1)} %all-gather.8.cloned.1.call-done, f32[2,1536,768]{1,2,0:T(8,128)} %reshape.301, f32[2,1536]{1,0:T(2,128)S(1)} %bitcast.109), kind=kOutput, calls=%fused_computation | convolution fusion | flops 14528544768 | bytes 56635392 | tf_op jit(solution)/shard_map/erd,efd->erf/dot_general | solution.py:356
  378.8 20.8 %convolution_convert_fusion.6 = bf16[2,1536,768]{2,1,0:T(8,128)(2,1)S(1)} fusion(bf16[2,1536,3072]{2,1,0:T(8,128)(2,1)} %multiply_convert_fusion, bf16[2,768,3072]{2,1,0:T(8,128)(2,1)} %all-gather.6.cloned.1.call-done.up_ref), kind=kOutput, calls=%fused_computation.34 | convolution fusion | flops 14497873920 | bytes 33030144 | tf_op jit(solution)/shard_map/erf,edf->erd/dot_general | solution.py:360
  402.1 5.1 all-to-all-start.3
  409.9 3.3 fusion.34
  413.2 98.0 %all-to-all-done.3 = bf16[2,4,384,768]{3,2,0,1:T(8,128)(2,1)} async-done(((bf16[2,4,384,768]{3,2,0,1:T(8,128)(2,1)}), bf16[2,4,384,768]{3,2,0,1:T(8,128)(2,1)}, u32[]{:S(2)}, u32[]{:S(2)}) %all-to-all-start.3) | async-done | bytes 4718624 | tf_op jit(solution)/shard_map/all_to_all | solution.py:243
  511.1 9.1 multiply_reduce_fusion.1
  521.0 4.8 convolution_convert_fusion.8.go_ref
  525.8 34.5 %shard_map.222 = (bf16[1024,768]{1,0:T(8,128)(2,1)S(1)}, bf16[1024,768]{1,0:T(8,128)(2,1)S(1)}, bf16[1024,768]{1,0:T(8,128)(2,1)S(1)}, f32[12,384,128]{2,1,0:T(8,128)}) custom-call(bf16[1024,2304]{1,0:T(8,128)(2,1)} %convolution_convert_fusion.2.q_ref.k_ref.v_ref, bf16[1024,2304]{1,0:T(8,128)(2,1)} %convolution_convert_fusion.2.q_ref.k_ref.v_ref, ...), custom_call_target="tpu_custom_call" | custom-call | tf_op jit(solution)/shard_map/pallas_call | solution.py:157
  561.5 2.8 slice.96
  568.1 3.0 copy.137
  571.1 4.0 fusion.27
  578.8 4.2 convolution_convert_fusion.3
  583.1 6.4 fusion.18
  591.8 3.8 fusion.7
  596.3 25.1 %convolution_convert_fusion.1 = bf16[2,3072,768]{2,1,0:T(8,128)(2,1)} fusion(bf16[2,1536,3072]{2,1,0:T(8,128)(2,1)} %get-tuple-element.23, f32[2,1536,768]{1,2,0:T(8,128)} %reshape.301, f32[2,1536]{1,0:T(2,128)S(1)} %bitcast.110), kind=kOutput, calls=%fused_computation.16 | convolution fusion | flops 14504951808 | bytes 37761024 | tf_op jit(solution)/shard_map/erf,erd->efd/dot_general | solution.py:364
  621.5 21.7 %convolution_convert_fusion = bf16[2,768,3072]{2,1,0:T(8,128)(2,1)} fusion(bf16[2,1536,768]{2,1,0:T(8,128)(2,1)} %bitcast.92, bf16[2,1536,3072]{2,1,0:T(8,128)(2,1)} %multiply_convert_fusion), kind=kOutput, calls=%fused_computation.15 | convolution fusion | flops 14500233216 | bytes 33030144 | tf_op jit(solution)/shard_map/erd,erf->edf/dot_general | solution.py:367
  643.2 9.1 reshape.294
  652.2 8.4 copy.128
  660.7 5.0 all-to-all-start.4
  666.4 85.9 %reduce-scatter.8.cloned.1.call-done = bf16[2,768,768]{2,1,0:T(8,128)(2,1)} async-done(((bf16[2,3072,768]{2,1,0:T(8,128)(2,1)}), bf16[2,768,768]{2,1,0:T(8,128)(2,1)}) %reduce-scatter.8.cloned.1.call-update) | async-done | bytes 2359312 | tf_op jit(solution)/shard_map/reduce_scatter | solution.py:370
  752.4 98.0 %reduce-scatter.6.cloned.1.call-done = bf16[2,768,768]{2,1,0:T(8,128)(2,1)} async-done(((bf16[2,768,3072]{2,1,0:T(8,128)(2,1)}), bf16[2,768,768]{2,1,0:T(8,128)(2,1)}) %reduce-scatter.6.cloned.1.call-update) | async-done | bytes 2359312 | tf_op jit(solution)/shard_map/reduce_scatter | solution.py:371
  850.5 4.9 fusion.4
  857.9 4.0 copy.144
  861.8 9.5 add_convert_fusion
  873.9 36.9 %all-reduce.10.cloned.1.call-done = bf16[192,3200]{1,0:T(8,128)(2,1)} async-done(((bf16[192,3200]{1,0:T(8,128)(2,1)}), bf16[192,3200]{1,0:T(8,128)(2,1)}) %all-reduce.10.cloned.1.call-update) | async-done | bytes 1228816 | tf_op jit(solution)/shard_map/psum | solution.py:425
  918.6 25.1 %all-reduce.12.cloned.1.call-done = (bf16[2,768,768]{2,1,0:T(8,128)(2,1)}, bf16[2,768,768]{2,1,0:T(8,128)(2,1)}) async-done(((bf16[2,768,768]{2,1,0:T(8,128)(2,1)}, bf16[2,768,768]{2,1,0:T(8,128)(2,1)}), (bf16[2,768,768]{2,1,0:T(8,128)(2,1)}, bf16[2,768,768]{2,1,0:T(8,128)(2,1)})) %all-reduce.12.cloned.1.call-update) | async-done | bytes 4718608 | tf_op jit(solution)/shard_map/psum | solution.py:371
  943.8 4.4 convert_element_type.339
  (192 shorter events, 66.9 us)
Async XLA Ops:
  7.2 8.8 copy-start.30
  7.2 69.0 %all-gather.4.cloned.1.call-start = ((), (), s32[]{:S(2)}) async-start(), calls=%async_computation.9 | async-start | bytes 6144000 | tf_op jit(solution)/shard_map/all_gather | solution.py:282
  15.2 3.6 copy-start.21
  15.2 240.7 %all-gather.6.cloned.1.call-start = ((), (), s32[]{:S(2)}) async-start(), calls=%async_computation.10 | async-start | bytes 11796480 | tf_op jit(solution)/shard_map/all_gather | solution.py:285
  16.9 494.2 %copy-start.25 = (s32[8,1024]{1,0:T(8,128)}, s32[8,1024]{1,0:T(8,128)S(1)}, u32[]{:S(2)}) copy-start(s32[8,1024]{1,0:T(8,128)S(1)} %fusion.25) | copy-start | bytes 98308
  18.8 6.7 copy-start.14
  32.3 5.6 copy-start.19
  32.3 109.7 %all-to-all-start.1 = ((bf16[4,2,384,768]{2,3,1,0:T(8,128)(2,1)}), bf16[4,2,384,768]{2,3,1,0:T(8,128)(2,1)}, u32[]{:S(2)}, u32[]{:S(2)}) async-start(bf16[4,2,384,768]{2,3,1,0:T(8,128)(2,1)} %copy.123), calls=%async_computation.1 | async-start | bytes 9437184 | tf_op jit(solution)/shard_map/all_to_all | solution.py:236
  37.7 273.0 %all-gather.8.cloned.1.call-start = ((), (), s32[]{:S(2)}) async-start(), calls=%async_computation.11 | async-start | bytes 11796480 | tf_op jit(solution)/shard_map/all_gather | solution.py:286
  49.8 63.2 %copy-start.4 = (bf16[1024,768]{0,1:T(8,128)(2,1)}, bf16[1024,768]{0,1:T(8,128)(2,1)S(1)}, u32[]{:S(2)}) copy-start(bf16[1024,768]{0,1:T(8,128)(2,1)S(1)} %copy.115) | copy-start | bytes 4718596
  50.2 32.5 %copy-start.33 = (f32[1024]{0:T(1024)}, f32[1024]{0:T(1024)S(1)}, u32[]{:S(2)}) copy-start(f32[1024]{0:T(1024)S(1)} %add_rsqrt_fusion.1) | copy-start | bytes 12292
  78.8 3.8 copy-start.31
  79.5 3.2 slice-start
  80.1 3.0 slice-start.1
  114.5 3.0 copy-start.15
  142.0 109.1 %all-to-all-start = ((bf16[4,2,384,768]{3,2,1,0:T(8,128)(2,1)}), bf16[4,2,384,768]{3,2,1,0:T(8,128)(2,1)}, u32[]{:S(2)}, u32[]{:S(2)}) async-start(bf16[4,2,384,768]{3,2,1,0:T(8,128)(2,1)} %bitcast.95), calls=%async_computation | async-start | bytes 9437184 | tf_op jit(solution)/shard_map/all_to_all | solution.py:236
  256.0 2.3 copy-start
  334.8 7.7 all-to-all-start.5
  338.0 40.7 %copy-start.27 = (f32[8,1024]{1,0:T(8,128)}, f32[8,1024]{1,0:T(8,128)S(1)}, u32[]{:S(2)}) copy-start(f32[8,1024]{1,0:T(8,128)S(1)} %select_reduce_fusion) | copy-start | bytes 98308
  353.0 25.8 %copy-start.37 = (f32[4,2,384]{2,1,0:T(2,128)}, f32[4,2,384]{2,1,0:T(2,128)S(1)}, u32[]{:S(2)}) copy-start(f32[4,2,384]{2,1,0:T(2,128)S(1)} %all_to_all.84) | copy-start | bytes 36868
  402.1 5.2 copy-start.22
  402.1 109.0 %all-to-all-start.3 = ((bf16[2,4,384,768]{3,2,0,1:T(8,128)(2,1)}), bf16[2,4,384,768]{3,2,0,1:T(8,128)(2,1)}, u32[]{:S(2)}, u32[]{:S(2)}) async-start(bf16[2,4,384,768]{3,2,0,1:T(8,128)(2,1)} %copy.127), calls=%async_computation.3 | async-start | bytes 9437184 | tf_op jit(solution)/shard_map/all_to_all | solution.py:243
  407.2 2.1 copy-start.29
  407.2 258.5 %reduce-scatter.4.cloned.1.call-start = ((), (), s32[]{:S(2)}) async-start(), calls=%async_computation.12 | async-start | bytes 6144000 | tf_op jit(solution)/shard_map/reduce_scatter | solution.py:424
  409.9 101.3 %copy-start.8 = (f32[1024,768]{0,1:T(8,128)S(1)}, f32[1024,768]{0,1:T(8,128)}, u32[]{:S(2)}) copy-start(f32[1024,768]{0,1:T(8,128)} %copy-done.7) | copy-start | bytes 9437188
  511.1 9.1 copy-start.13
  521.0 44.6 %copy-start.10 = (f32[1024,768]{0,1:T(8,128)}, f32[1024,768]{0,1:T(8,128)S(1)}, u32[]{:S(2)}) copy-start(f32[1024,768]{0,1:T(8,128)S(1)} %multiply_add_fusion) | copy-start | bytes 9437188
  561.5 4.1 copy-start.3
  568.1 3.0 copy-start.24
  577.4 5.6 slice-start.2
  578.8 4.3 slice-start.3
  583.1 6.4 copy-start.40
  583.1 6.4 copy-start.36
  595.6 156.8 %reduce-scatter.8.cloned.1.call-start = ((), (), s32[]{:S(2)}) async-start(), calls=%async_computation.15 | async-start | bytes 11796480 | tf_op jit(solution)/shard_map/reduce_scatter | solution.py:370
  621.4 229.0 %reduce-scatter.6.cloned.1.call-start = ((), (), s32[]{:S(2)}) async-start(), calls=%async_computation.14 | async-start | bytes 11796480 | tf_op jit(solution)/shard_map/reduce_scatter | solution.py:371
  660.7 201.2 %all-to-all-start.4 = ((bf16[2,4,384,768]{3,2,0,1:T(8,128)(2,1)}), bf16[2,4,384,768]{3,2,0,1:T(8,128)(2,1)}, u32[]{:S(2)}, u32[]{:S(2)}) async-start(bf16[2,4,384,768]{3,2,0,1:T(8,128)(2,1)} %copy.128), calls=%async_computation.4 | async-start | bytes 9437184 | tf_op jit(solution)/shard_map/all_to_all | solution.py:243
  665.6 184.8 %copy-start.28 = (f32[8,1024]{1,0:T(8,128)S(1)}, f32[8,1024]{1,0:T(8,128)}, u32[]{:S(2)}) copy-start(f32[8,1024]{1,0:T(8,128)} %copy-done.27) | copy-start | bytes 98308
  665.6 184.8 %copy-start.26 = (s32[8,1024]{1,0:T(8,128)S(1)}, s32[8,1024]{1,0:T(8,128)}, u32[]{:S(2)}) copy-start(s32[8,1024]{1,0:T(8,128)} %copy-done.25) | copy-start | bytes 98308
  665.6 245.2 %all-reduce.10.cloned.1.call-start = ((), (), s32[]{:S(2)}) async-start(), calls=%async_computation.13 | async-start | bytes 2457600 | tf_op jit(solution)/shard_map/psum | solution.py:425
  666.4 277.4 %all-reduce.12.cloned.1.call-start = ((), (), s32[]{:S(2)}) async-start(), calls=%async_computation.16 | async-start | bytes 9437184 | tf_op jit(solution)/shard_map/psum | solution.py:371
  850.4 5.0 copy-start.16
  850.4 5.0 copy-start.39
  850.4 4.9 copy-start.6
  850.4 4.9 copy-start.11
  850.5 4.9 copy-start.35
  857.9 4.0 copy-start.9
  910.9 3.9 copy-start.12
  943.8 4.4 copy-start.18
  (10 other events, 12.4 us)
Sparse Core Ops, SparseCore 0:
  15.3 60.7 all-gather.3
  78.0 96.3 all-gather.5
  176.2 96.3 all-gather.7
  595.8 58.6 reduce-scatter.3
  657.4 94.9 reduce-scatter.7
  755.3 94.9 reduce-scatter.5
  852.7 58.1 all-reduce.9
  913.4 30.2 all-reduce.11
